TPU v7x, 512 devices: a whole 4x8x8 slice. The times are simulated.
512 devices in a mesh: seq: 64 (over y, z_hi, core), head: 8 (over x, z_lo).
Axes of the slice: x: 4, y: 8, z: 8 (z_hi: 4, z_lo: 2; z = z_hi * 2 + z_lo), core: 2. Of those that a mesh axis runs over, the one named last changes fastest.
Arguments:
- queries: bfloat16 [8192, 8192], P(('seq', 'head')), may hold values from -6 to 6, as said below
- response_keys: bfloat16 [8192, 1024], P(('seq', 'head')), may hold values from -6 to 6
- response_values: bfloat16 [8192, 1024], P(('seq', 'head')), may hold values from -96 to 96
- shared_prompt_keys: bfloat16 [512, 1024], P('seq', 'head'), may hold values from -6 to 6
- shared_prompt_values: bfloat16 [512, 1024], P('seq', 'head'), may hold values from -96 to 96
- output_gradient: bfloat16 [8192, 8192], P(('seq', 'head')), may hold values from -24 to 24
- lengths: int32 [8], replicated, may hold values from 1 to 1024, 5120 in all
Outputs:
- attended: bfloat16 [8192, 8192], P('seq', 'head')
- query_grad: bfloat16 [8192, 8192], P('seq', 'head')
- response_key_gradient: bfloat16 [8192, 1024], P('seq', 'head')
- response_value_gradient: bfloat16 [8192, 1024], P('seq', 'head')
- prompt_key_gradient: float32 [512, 1024], P('seq', 'head')
- prompt_value_gradient: float32 [512, 1024], P('seq', 'head')
Inputs may be any that keep to these rules, and one draw needn't show every extreme that they name: At the first position of each response, in the hidden draw, some queries may be large multiples of a fixed sign pattern. `lengths`: the longest response has exactly 1024 tokens.
All inputs are finite; a program needn't handle non-finite values.
Results may differ from a plain program's by a relative error of at most 0.03.
Values may be sent and summed in bfloat16 or wider, within the bound.
A program may use at most 64 MiB of HBM per device.

v0:
```python
import math

import jax
import jax.numpy as jnp
from jax import lax
from jax.sharding import PartitionSpec as P

QUERY_HEADS = 64
KEY_VALUE_HEADS = 8
HEAD_WIDTH = 128
RESPONSE_LENGTH = 1024


def from_behind(block, axis, distance):
    devices = range(lax.axis_size(axis))
    route = [(i - distance, i) for i in devices if i - distance in devices]
    return lax.ppermute(block, axis, route)


def attend_scores(queries4, block_keys, key_mask, score_scale):
    scores = (
        jnp.einsum("tkgd,ckd->tkgc", queries4, block_keys, preferred_element_type=jnp.float32)
        * score_scale
    )
    if key_mask is None:
        return scores
    return jnp.where(key_mask[:, None, None, :], scores, -jnp.inf)


def block_grads(
    queries4, grads4, block_keys, block_values, key_mask, log_total, delta, score_scale
):
    scores = attend_scores(queries4, block_keys, key_mask, score_scale)
    weights = jnp.exp(scores - log_total[..., None])
    weights_bf = weights.astype(jnp.bfloat16)
    dweights = jnp.einsum(
        "tkgd,ckd->tkgc", grads4, block_values, preferred_element_type=jnp.float32
    )
    dscores = (weights * (dweights - delta[..., None])).astype(jnp.bfloat16)
    query_term = jnp.einsum(
        "tkgc,ckd->tkgd", dscores, block_keys, preferred_element_type=jnp.float32
    )
    key_term = (
        jnp.einsum("tkgc,tkgd->ckd", dscores, queries4, preferred_element_type=jnp.float32)
        * score_scale
    )
    value_term = jnp.einsum(
        "tkgc,tkgd->ckd", weights_bf, grads4, preferred_element_type=jnp.float32
    )
    return (query_term, key_term, value_term)


def per_device(
    queries,
    response_keys,
    response_values,
    shared_prompt_keys,
    shared_prompt_values,
    output_gradient,
    lengths,
):
    head_queries, head_keys, head_values, head_grads = (
        lax.all_to_all(queries, "head", split_axis=1, concat_axis=0, tiled=True),
        lax.all_to_all(response_keys, "head", split_axis=1, concat_axis=0, tiled=True),
        lax.all_to_all(response_values, "head", split_axis=1, concat_axis=0, tiled=True),
        lax.all_to_all(output_gradient, "head", split_axis=1, concat_axis=0, tiled=True),
    )
    tok_rows = head_queries.shape[0]
    kv_local = head_keys.shape[1] // HEAD_WIDTH
    group_count = QUERY_HEADS // KEY_VALUE_HEADS
    span_count = RESPONSE_LENGTH // tok_rows
    score_scale = HEAD_WIDTH ** (-0.5)
    seq_index = lax.axis_index("seq")
    resp_index = seq_index * tok_rows // RESPONSE_LENGTH
    length = jnp.sum(jnp.where(jnp.arange(lengths.shape[0]) == resp_index, lengths, 0))
    query_pos = seq_index * tok_rows - resp_index * RESPONSE_LENGTH + jnp.arange(tok_rows)
    live_rows = query_pos < length
    queries4 = head_queries.reshape(tok_rows, kv_local, group_count, HEAD_WIDTH)
    grads4 = (
        head_grads.reshape(tok_rows, kv_local, group_count, HEAD_WIDTH)
        * live_rows.astype(jnp.bfloat16)[:, None, None, None]
    )
    prompt_all_keys, prompt_all_values = (
        lax.all_gather(shared_prompt_keys, "seq", axis=0, tiled=True),
        lax.all_gather(shared_prompt_values, "seq", axis=0, tiled=True),
    )
    prompt_total = prompt_all_keys.shape[0]
    prompt_block = math.gcd(prompt_total, 256)
    blocks = []
    for first_row in range(0, prompt_total, prompt_block):
        blocks.append(
            (
                prompt_all_keys[first_row : first_row + prompt_block].reshape(
                    prompt_block, kv_local, HEAD_WIDTH
                ),
                prompt_all_values[first_row : first_row + prompt_block].reshape(
                    prompt_block, kv_local, HEAD_WIDTH
                ),
                None,
                -1,
            )
        )
    key_pair = jnp.stack([head_keys, head_values])
    for shifted_by in range(span_count - 1, -1, -1):
        if shifted_by > 0:
            moved = from_behind(key_pair, "seq", shifted_by)
        else:
            moved = key_pair
        key_pos = (
            (seq_index - shifted_by) * tok_rows
            - resp_index * RESPONSE_LENGTH
            + jnp.arange(tok_rows)
        )
        key_mask = (
            (key_pos[None, :] >= 0)
            & (key_pos[None, :] <= query_pos[:, None])
            & (key_pos[None, :] < length)
        )
        blocks.append(
            (
                moved[0].reshape(tok_rows, kv_local, HEAD_WIDTH),
                moved[1].reshape(tok_rows, kv_local, HEAD_WIDTH),
                key_mask,
                shifted_by,
            )
        )
    top_score = jnp.full((tok_rows, kv_local, group_count), -jnp.inf, jnp.float32)
    exp_total = jnp.zeros((tok_rows, kv_local, group_count), jnp.float32)
    for block_keys, block_values, key_mask, shifted_by in blocks:
        scores = attend_scores(queries4, block_keys, key_mask, score_scale)
        new_top = jnp.maximum(top_score, jnp.max(scores, axis=-1))
        exp_total = exp_total * jnp.exp(top_score - new_top) + jnp.sum(
            jnp.exp(scores - new_top[..., None]), axis=-1
        )
        top_score = new_top
    log_total = top_score + jnp.log(exp_total)
    out_acc = jnp.zeros((tok_rows, kv_local, group_count, HEAD_WIDTH), jnp.float32)
    for block_keys, block_values, key_mask, shifted_by in blocks:
        scores = attend_scores(queries4, block_keys, key_mask, score_scale)
        weights_bf = jnp.exp(scores - log_total[..., None]).astype(jnp.bfloat16)
        out_acc = out_acc + jnp.einsum(
            "tkgc,ckd->tkgd", weights_bf, block_values, preferred_element_type=jnp.float32
        )
    attended4 = (out_acc * live_rows.astype(jnp.float32)[:, None, None, None]).astype(jnp.bfloat16)
    delta = jnp.sum(grads4.astype(jnp.float32) * attended4.astype(jnp.float32), axis=-1)
    query_acc = jnp.zeros((tok_rows, kv_local, group_count, HEAD_WIDTH), jnp.float32)
    own_total = jnp.zeros((2, tok_rows, kv_local, HEAD_WIDTH), jnp.float32)
    prompt_key_terms = []
    prompt_value_terms = []
    for block_keys, block_values, key_mask, shifted_by in blocks:
        query_term, key_term, value_term = block_grads(
            queries4, grads4, block_keys, block_values, key_mask, log_total, delta, score_scale
        )
        query_acc = query_acc + query_term
        if shifted_by < 0:
            prompt_key_terms.append(key_term)
            prompt_value_terms.append(value_term)
        else:
            term_pair = jnp.stack([key_term, value_term])
            if shifted_by > 0:
                term_pair = from_behind(term_pair.astype(jnp.bfloat16), "seq", -shifted_by).astype(
                    term_pair.dtype
                )
            own_total = own_total + term_pair
    prompt_key_all = jnp.concatenate(prompt_key_terms, axis=0).reshape(
        prompt_total, kv_local * HEAD_WIDTH
    )
    prompt_value_all = jnp.concatenate(prompt_value_terms, axis=0).reshape(
        prompt_total, kv_local * HEAD_WIDTH
    )
    prompt_key_gradient, prompt_value_gradient = (
        lax.psum_scatter(prompt_key_all, "seq", scatter_dimension=0, tiled=True),
        lax.psum_scatter(prompt_value_all, "seq", scatter_dimension=0, tiled=True),
    )
    attended_out = attended4.reshape(tok_rows, kv_local * group_count * HEAD_WIDTH)
    query_grad = (
        (query_acc * score_scale)
        .astype(jnp.bfloat16)
        .reshape(tok_rows, kv_local * group_count * HEAD_WIDTH)
    )
    response_key_gradient = (
        own_total[0].astype(jnp.bfloat16).reshape(tok_rows, kv_local * HEAD_WIDTH)
    )
    response_value_gradient = (
        own_total[1].astype(jnp.bfloat16).reshape(tok_rows, kv_local * HEAD_WIDTH)
    )
    return (
        attended_out,
        query_grad,
        response_key_gradient,
        response_value_gradient,
        prompt_key_gradient,
        prompt_value_gradient,
    )


def solution(mesh):
    return jax.shard_map(
        per_device,
        mesh=mesh,
        in_specs=(
            P(("seq", "head"), None),
            P(("seq", "head"), None),
            P(("seq", "head"), None),
            P("seq", "head"),
            P("seq", "head"),
            P(("seq", "head"), None),
            P(),
        ),
        out_specs=(
            P("seq", "head"),
            P("seq", "head"),
            P("seq", "head"),
            P("seq", "head"),
            P("seq", "head"),
            P("seq", "head"),
        ),
        check_vma=False,
    )
```

profile of v0, /device:TPU:1, one launch (start us, length us, event | category | flops | bytes accessed | tf_op | source)
XLA Modules:
  0.0 900.6 jit_solution(17672588625764620936)
XLA Ops:
  8.6 6.7 all-to-all-start.1
  19.9 1.4 copy_bitcast_fusion.2
  22.2 5.2 all-to-all-start.2
  27.4 88.8 %all_gather.6 = bf16[512,128]{1,0:T(8,128)(2,1)S(1)} all-gather(bf16[8,128]{1,0:T(8,128)(2,1)S(1)} %copy-done.71), channel_id=1, replica_groups=mesh['seq'=64,'head'=8] {'seq'}, dimensions={0}, use_global_device_ids=true | all-gather | bytes 133120 | tf_op jit(solution)/shard_map/all_gather | solution.py:84
  116.2 5.6 all-to-all-start
  121.8 80.2 %all_gather.7 = bf16[512,128]{1,0:T(8,128)(2,1)} all-gather(bf16[8,128]{1,0:T(8,128)(2,1)S(1)} %copy-done.72), channel_id=1, replica_groups=mesh['seq'=64,'head'=8] {'seq'}, dimensions={0}, use_global_device_ids=true | all-gather | bytes 133120 | tf_op jit(solution)/shard_map/all_gather | solution.py:85
  206.4 5.3 collective-permute-start.6
  211.7 1.9 collective-permute-start.5
  213.6 1.3 collective-permute-start.4
  214.9 4.3 collective-permute-start.3
  219.3 1.3 collective-permute-start
  220.6 5.5 all-to-all-start.3
  226.4 4.5 collective-permute-start.1
  231.2 2.2 collective-permute-done.1
  233.4 7.7 collective-permute-start.2
  249.2 1.7 fusion.149
  251.8 1.8 copy.329
  253.7 2.2 copy.389
  255.9 2.2 copy.388
  258.1 1.4 fusion.151
  260.6 1.8 copy.363
  262.5 1.8 copy.366
  264.3 1.8 copy.369
  266.1 1.8 copy.372
  267.9 1.8 copy.375
  269.8 1.8 copy.378
  271.6 1.8 copy.381
  273.4 1.8 copy.384
  322.8 2.2 collective-permute-start.13
  328.3 2.5 collective-permute-done.13
  330.8 8.6 collective-permute-done.7
  341.0 549.9 %all-reduce.5.cloned.1.call-done = (f32[512,128]{1,0:T(8,128)}, f32[512,128]{0,1:T(8,128)}) async-done(((f32[512,128]{1,0:T(8,128)}, f32[512,128]{0,1:T(8,128)}), (f32[512,128]{1,0:T(8,128)}, f32[512,128]{0,1:T(8,128)})) %all-reduce.5.cloned.1.call-update) | async-done | bytes 524304
  (285 shorter events, 75.7 us)
Async XLA Ops:
  7.2 14.1 %copy-start.68 = (bf16[16,8192]{1,0:T(8,128)(2,1)S(1)}, bf16[16,8192]{1,0:T(8,128)(2,1)}, u32[]{:S(2)}) copy-start(bf16[16,8192]{1,0:T(8,128)(2,1)} %param.7) | copy-start | bytes 786436
  8.6 13.7 %all-to-all-start.1 = ((bf16[16,8,128]{2,0,1:T(8,128)(2,1)}), bf16[16,8,128]{2,0,1:T(8,128)(2,1)S(1)}, u32[]{:S(2)}, u32[]{:S(2)}) async-start(bf16[16,8,128]{2,0,1:T(8,128)(2,1)} %copy_bitcast_fusion.3), calls=%async_computation.1 | async-start | bytes 65536 | tf_op jit(solution)/shard_map/all_to_all | solution.py:64
  22.2 5.2 copy-start.71
  22.2 94.0 %all-to-all-start.2 = ((bf16[16,8,128]{2,0,1:T(8,128)(2,1)}), bf16[16,8,128]{2,0,1:T(8,128)(2,1)S(1)}, u32[]{:S(2)}, u32[]{:S(2)}) async-start(bf16[16,8,128]{2,0,1:T(8,128)(2,1)} %copy_bitcast_fusion.2), calls=%async_computation.2 | async-start | bytes 65536 | tf_op jit(solution)/shard_map/all_to_all | solution.py:65
  116.2 129.7 %copy-start.27 = (bf16[512,128]{1,0:T(8,128)(2,1)}, bf16[512,128]{1,0:T(8,128)(2,1)S(1)}, u32[]{:S(2)}) copy-start(bf16[512,128]{1,0:T(8,128)(2,1)S(1)} %all_gather.6) | copy-start | bytes 393220
  116.2 5.6 copy-start.72
  116.2 85.8 %copy-start.69 = (bf16[16,8192]{1,0:T(8,128)(2,1)S(1)}, bf16[16,8192]{1,0:T(8,128)(2,1)}, u32[]{:S(2)}) copy-start(bf16[16,8192]{1,0:T(8,128)(2,1)} %param.12) | copy-start | bytes 786436
  116.2 104.3 %all-to-all-start = ((bf16[16,8,1024]{2,0,1:T(8,128)(2,1)}), bf16[16,8,1024]{2,0,1:T(8,128)(2,1)S(1)}, u32[]{:S(2)}, u32[]{:S(2)}) async-start(bf16[16,8,1024]{2,0,1:T(8,128)(2,1)} %bitcast.834), calls=%async_computation | async-start | bytes 524288 | tf_op jit(solution)/shard_map/all_to_all | solution.py:63
  206.4 39.8 %collective-permute-start.6 = (bf16[2,128,128]{2,1,0:T(8,128)(2,1)}, bf16[2,128,128]{2,1,0:T(8,128)(2,1)S(1)}, u32[]{:S(2)}, u32[]{:S(2)}) collective-permute-start(bf16[2,128,128]{2,1,0:T(8,128)(2,1)} %pad_maximum_fusion), channel_id=1, source_target_pairs={{0,8},{8,16},{16,24},{24,32},{32,40},{40,48},{48,56},{56,64},{64,7... | collective-permute-start | bytes 196616 | tf_op jit(solution)/shard_map/ppermute | solution.py:17
  211.7 33.3 %collective-permute-start.5 = (bf16[2,128,128]{2,1,0:T(8,128)(2,1)}, bf16[2,128,128]{2,1,0:T(8,128)(2,1)S(1)}, u32[]{:S(2)}, u32[]{:S(2)}) collective-permute-start(bf16[2,128,128]{2,1,0:T(8,128)(2,1)} %pad_maximum_fusion), channel_id=1, source_target_pairs={{0,16},{8,24},{16,32},{24,40},{32,48},{40,56},{48,64},{56,72},{64,... | collective-permute-start | bytes 196616 | tf_op jit(solution)/shard_map/ppermute | solution.py:17
  213.6 30.6 %collective-permute-start.4 = (bf16[2,128,128]{2,1,0:T(8,128)(2,1)}, bf16[2,128,128]{2,1,0:T(8,128)(2,1)S(1)}, u32[]{:S(2)}, u32[]{:S(2)}) collective-permute-start(bf16[2,128,128]{2,1,0:T(8,128)(2,1)} %pad_maximum_fusion), channel_id=1, source_target_pairs={{0,24},{8,32},{16,40},{24,48},{32,56},{40,64},{48,72},{56,80},{64,... | collective-permute-start | bytes 196616 | tf_op jit(solution)/shard_map/ppermute | solution.py:17
  214.9 28.3 %collective-permute-start.3 = (bf16[2,128,128]{2,1,0:T(8,128)(2,1)}, bf16[2,128,128]{2,1,0:T(8,128)(2,1)S(1)}, u32[]{:S(2)}, u32[]{:S(2)}) collective-permute-start(bf16[2,128,128]{2,1,0:T(8,128)(2,1)} %pad_maximum_fusion), channel_id=1, source_target_pairs={{0,32},{8,40},{16,48},{24,56},{32,64},{40,72},{48,80},{56,88},{64,... | collective-permute-start | bytes 196616 | tf_op jit(solution)/shard_map/ppermute | solution.py:17
  219.3 7.1 collective-permute-start
  220.6 30.4 %all-to-all-start.3 = ((bf16[16,8,1024]{2,0,1:T(8,128)(2,1)}), bf16[16,8,1024]{2,0,1:T(8,128)(2,1)S(1)}, u32[]{:S(2)}, u32[]{:S(2)}) async-start(bf16[16,8,1024]{2,0,1:T(8,128)(2,1)} %bitcast.833), calls=%async_computation.3 | async-start | bytes 524288 | tf_op jit(solution)/shard_map/all_to_all | solution.py:66
  226.0 664.8 %all-reduce.5.cloned.1.call-start = ((), (), s32[]{:S(2)}) async-start(), calls=%async_computation.4 | async-start | bytes 1048576
  226.4 22.8 %copy-start.7 = (f32[128,1,8,128]{0,3,2,1:T(8,128)}, f32[128,1,8,128]{0,3,2,1:T(8,128)S(1)}, u32[]{:S(2)}) copy-start(f32[128,1,8,128]{0,3,2,1:T(8,128)S(1)} %get-tuple-element.64) | copy-start | bytes 1572868
  226.4 4.8 copy-start.47
  226.4 7.0 collective-permute-start.1
  231.2 17.9 %copy-start.1 = (f32[128,1,8,128]{0,3,2,1:T(8,128)}, f32[128,1,8,128]{0,3,2,1:T(8,128)S(1)}, u32[]{:S(2)}) copy-start(f32[128,1,8,128]{0,3,2,1:T(8,128)S(1)} %get-tuple-element.78) | copy-start | bytes 1572868
  233.4 8.0 copy-start.62
  233.4 9.2 %collective-permute-start.2 = (bf16[2,128,128]{2,1,0:T(8,128)(2,1)}, bf16[2,128,128]{2,1,0:T(8,128)(2,1)S(1)}, u32[]{:S(2)}, u32[]{:S(2)}) collective-permute-start(bf16[2,128,128]{2,1,0:T(8,128)(2,1)} %pad_maximum_fusion), channel_id=1, source_target_pairs={{0,40},{8,48},{16,56},{24,64},{32,72},{40,80},{48,88},{56,96},{64,... | collective-permute-start | bytes 196616 | tf_op jit(solution)/shard_map/ppermute | solution.py:17
  243.2 5.9 copy-start.3
  243.9 5.3 copy-start.5
  244.8 4.3 copy-start.9
  304.7 18.0 %collective-permute-start.8 = (bf16[2,128,1,128]{3,1,2,0:T(8,128)(2,1)}, bf16[2,128,1,128]{3,1,2,0:T(8,128)(2,1)S(1)}, u32[]{:S(2)}, u32[]{:S(2)}) collective-permute-start(bf16[2,128,1,128]{3,1,2,0:T(8,128)(2,1)} %pad_maximum_fusion.2), channel_id=1, source_target_pairs={{48,0},{56,8},{64,16},{72,24},{80,32},{88,40},{96,48},{104,56},{11... | collective-permute-start | bytes 196616 | tf_op jit(solution)/shard_map/ppermute | solution.py:17
  306.7 18.3 %collective-permute-start.9 = (bf16[2,128,1,128]{3,1,2,0:T(8,128)(2,1)}, bf16[2,128,1,128]{3,1,2,0:T(8,128)(2,1)S(1)}, u32[]{:S(2)}, u32[]{:S(2)}) collective-permute-start(bf16[2,128,1,128]{3,1,2,0:T(8,128)(2,1)} %pad_maximum_fusion.3), channel_id=1, source_target_pairs={{40,0},{48,8},{56,16},{64,24},{72,32},{80,40},{88,48},{96,56},{104... | collective-permute-start | bytes 196616 | tf_op jit(solution)/shard_map/ppermute | solution.py:17
  308.6 19.7 %collective-permute-start.10 = (bf16[2,128,1,128]{3,1,2,0:T(8,128)(2,1)}, bf16[2,128,1,128]{3,1,2,0:T(8,128)(2,1)S(1)}, u32[]{:S(2)}, u32[]{:S(2)}) collective-permute-start(bf16[2,128,1,128]{3,1,2,0:T(8,128)(2,1)} %pad_maximum_fusion.4), channel_id=1, source_target_pairs={{32,0},{40,8},{48,16},{56,24},{64,32},{72,40},{80,48},{88,56},{96,... | collective-permute-start | bytes 196616 | tf_op jit(solution)/shard_map/ppermute | solution.py:17
  310.5 17.7 %collective-permute-start.11 = (bf16[2,128,1,128]{3,1,2,0:T(8,128)(2,1)}, bf16[2,128,1,128]{3,1,2,0:T(8,128)(2,1)S(1)}, u32[]{:S(2)}, u32[]{:S(2)}) collective-permute-start(bf16[2,128,1,128]{3,1,2,0:T(8,128)(2,1)} %pad_maximum_fusion.5), channel_id=1, source_target_pairs={{24,0},{32,8},{40,16},{48,24},{56,32},{64,40},{72,48},{80,56},{88,... | collective-permute-start | bytes 196616 | tf_op jit(solution)/shard_map/ppermute | solution.py:17
  312.4 15.8 %collective-permute-start.12 = (bf16[2,128,1,128]{3,1,2,0:T(8,128)(2,1)}, bf16[2,128,1,128]{3,1,2,0:T(8,128)(2,1)}, u32[]{:S(2)}, u32[]{:S(2)}) collective-permute-start(bf16[2,128,1,128]{3,1,2,0:T(8,128)(2,1)} %pad_maximum_fusion.6), channel_id=1, source_target_pairs={{16,0},{24,8},{32,16},{40,24},{48,32},{56,40},{64,48},{72,56},{80,... | collective-permute-start | bytes 196616 | tf_op jit(solution)/shard_map/ppermute | solution.py:17
  322.0 4.3 copy-start.33
  322.8 8.0 collective-permute-start.13
  325.0 14.5 %collective-permute-start.7 = (bf16[2,128,1,128]{3,1,2,0:T(8,128)(2,1)S(1)}, bf16[2,128,1,128]{3,1,2,0:T(8,128)(2,1)S(1)}, u32[]{:S(2)}, u32[]{:S(2)}) collective-permute-start(bf16[2,128,1,128]{3,1,2,0:T(8,128)(2,1)S(1)} %pad_maximum_fusion.1), channel_id=1, source_target_pairs={{56,0},{64,8},{72,16},{80,24},{88,32},{96,40},{104,48},{112,56},{1... | collective-permute-start | bytes 196616 | tf_op jit(solution)/shard_map/ppermute | solution.py:17
  (60 other events, 63.9 us)
Sparse Core Ops, SparseCore 0:
  315.9 574.8 all-reduce.4
where the time goes:
time: 903 us; the launch traced here: 901 us
  waiting for transfers between devices  565 us (63%)
  blocking collectives  169 us (19%)
  starting transfers between devices  59.1 us (7%)
  local copies, waits for them, and re-layouts  55.6 us (6%)
  matrix products  20 us (2%)
  other arithmetic  16.5 us (2%)
  between operations  15.9 us (2%)
    unnamed x2, waiting for transfers between devices  550 us
    all_gather x1, blocking collectives, per_device(): lax.all_gather(shared_prompt_keys, 'seq', axis=0, tiled=True)  88.8 us
    all_gather x1, blocking collectives, per_device(): lax.all_gather(shared_prompt_values, 'seq', axis=0, tiled=True)  80.2 us
    ppermute x14, starting transfers between devices, from_behind(): return lax.ppermute(block, axis, route)  36.2 us
    unnamed x155, local copies, waits for them, and re-layouts  30.6 us
    another operation x10, local copies, waits for them, and re-layouts  19 us
  transfers between devices with their start and end apart: 19, of which 5 were waited for; matrix products, arithmetic and copies ran while one was open for 3% of the time, Pallas kernels for 0%

commit v1 on v0

v1 whole, which is shorter than its diff:
```python
import functools
import math

import jax
import jax.numpy as jnp
from jax import lax
from jax.experimental import pallas as pl
from jax.experimental.pallas import tpu as pltpu
from jax.sharding import PartitionSpec as P

MESH = pl.DeviceIdType.MESH
BF = jnp.bfloat16
F32 = jnp.float32
W = 128
G = 8
KB = 256
CB = 256
NEG = -1e30


def dot_nt(a, b):
    return lax.dot_general(a, b, (((1,), (1,)), ((), ())), preferred_element_type=F32)


def dot_nn(a, b):
    return lax.dot_general(a, b, (((1,), (0,)), ((), ())), preferred_element_type=F32)


def kernel(
    dims,
    q_hbm,
    k_hbm,
    v_hbm,
    pk_ref,
    pv_ref,
    do_hbm,
    len_ref,
    att_ref,
    dq_ref,
    dkv_ref,
    prom_ref,
    q_all,
    do_all,
    kvb,
    kvt,
    pg,
    qr,
    dor,
    dot_t,
    s_scr,
    p_scr,
    mx,
    lx,
    o_acc,
    dq_acc,
    acc,
    prom_s,
    prom_r,
    prom_y,
    prom_z,
    xs,
    xr,
    zs,
    zr,
    a2a_send,
    a2a_recv,
    own_sem,
    pz_send,
    pz_recv,
    py_send,
    py_recv,
    pc_send,
    pc_recv,
    kz_send,
    kz_recv,
    kc_send,
    kc_recv,
    gx_send,
    gx_recv,
    gz_send,
    gz_recv,
    rc_send,
    rc_recv,
    ry_send,
    ry_recv,
    rz_send,
    rz_recv,
):
    H, Y, Z, TR, U = dims
    T = H * TR
    R = T * G
    PT = U * Y * Z * 2
    NPB = PT // KB
    NC = R // CB
    GC = CB // T
    scale = W**-0.5
    c2 = scale * math.log2(math.e)

    s_me = lax.axis_index("seq")
    h = lax.axis_index("head")
    c = s_me % 2
    z = (s_me // 2) % Z
    y = s_me // (2 * Z)

    def at(yy, zz, cc, hh):
        return {"seq": (yy * Z + zz) * 2 + cc, "head": hh}

    def rcopy(src, dst, ssem, rsem, dev):
        return pltpu.make_async_remote_copy(
            src_ref=src, dst_ref=dst, send_sem=ssem, recv_sem=rsem, device_id=dev, device_id_type=MESH
        )

    other = at(y, z, 1 - c, h)

    unit = jnp.concatenate([pk_ref[...].astype(F32), pv_ref[...].astype(F32)], axis=0)
    pg[c, y, z] = unit.astype(BF)

    barrier = pltpu.get_barrier_semaphore()
    for d in range(1, H):
        pl.semaphore_signal(barrier, inc=1, device_id=at(y, z, c, (h + d) % H), device_id_type=MESH)
    for d in range(1, Y):
        pl.semaphore_signal(barrier, inc=1, device_id=at((y + d) % Y, z, c, h), device_id_type=MESH)
    for d in range(1, Z):
        pl.semaphore_signal(barrier, inc=1, device_id=at(y, (z + d) % Z, c, h), device_id_type=MESH)
    pl.semaphore_signal(barrier, inc=1, device_id=other, device_id_type=MESH)
    pl.semaphore_wait(barrier, H + Y + Z - 2)

    my_blk = NPB + z
    my_rows = pl.multiple_of(c * T, T)
    GW = G * W

    def src_dst(a, t, rows):
        row = pl.ds(pl.multiple_of(rows * TR, TR), TR)
        kv_row = pl.ds(pl.multiple_of(c * T + rows * TR, TR), TR)
        wide = pl.ds(pl.multiple_of(t * GW, GW), GW)
        thin = pl.ds(pl.multiple_of(t * W, W), W)
        if a == 0:
            return k_hbm.at[:, thin], kvb.at[my_blk, 0, kv_row, :]
        if a == 1:
            return v_hbm.at[:, thin], kvb.at[my_blk, 1, kv_row, :]
        if a == 2:
            return q_hbm.at[:, wide], q_all.at[row, :]
        return do_hbm.at[:, wide], do_all.at[row, :]

    def a2a_copy(a, d):
        t = (h + d) % H
        src, dst = src_dst(a, t, h)
        return rcopy(src, dst, a2a_send.at[a, d], a2a_recv.at[a, d], at(y, z, c, t))

    def own_copy(a):
        src, dst = src_dst(a, h, h)
        return pltpu.make_async_copy(src, dst, own_sem.at[a])

    def a2a_start(a):
        own_copy(a).start()
        for d in range(1, H):
            a2a_copy(a, d).start()

    def a2a_wait(a):
        own_copy(a).wait()
        for d in range(1, H):
            frm = (h + H - d) % H
            src, dst = src_dst(a, h, frm)
            rcopy(src, dst, a2a_send.at[a, d], a2a_recv.at[a, d], at(y, z, c, frm)).wait_recv()

    a2a_start(0)
    a2a_start(1)

    def pz_copy(d):
        return rcopy(
            pg.at[c, y, z], pg.at[c, y, z], pz_send.at[d], pz_recv.at[d], at(y, (z + d) % Z, c, h)
        )

    def pz_from(d):
        f = (z + Z - d) % Z
        return rcopy(pg.at[c, y, f], pg.at[c, y, f], pz_send.at[d], pz_recv.at[d], at(y, f, c, h))

    for d in range(1, Z):
        pz_copy(d).start()
    a2a_start(2)
    for d in range(1, Z):
        pz_from(d).wait_recv()

    def py_copy(d):
        return rcopy(pg.at[c, y], pg.at[c, y], py_send.at[d], py_recv.at[d], at((y + d) % Y, z, c, h))

    def py_from(d):
        f = (y + Y - d) % Y
        return rcopy(pg.at[c, f], pg.at[c, f], py_send.at[d], py_recv.at[d], at(f, z, c, h))

    for d in range(1, Y):
        py_copy(d).start()

    a2a_wait(0)
    a2a_wait(1)

    def span_ref(zz, cc):
        return kvb.at[NPB + zz, :, pl.ds(pl.multiple_of(cc * T, T), T), :]

    def kz_copy(d):
        return rcopy(
            span_ref(z, c), span_ref(z, c), kz_send.at[d], kz_recv.at[d], at(y, z + d, c, h)
        )

    def kz_from(d):
        return rcopy(
            span_ref(z - d, c), span_ref(z - d, c), kz_send.at[d], kz_recv.at[d], at(y, z - d, c, h)
        )

    def kc_copy(d):
        return rcopy(span_ref(z - d, c), span_ref(z - d, c), kc_send.at[d], kc_recv.at[d], other)

    def kc_from(d):
        return rcopy(
            span_ref(z - d, 1 - c), span_ref(z - d, 1 - c), kc_send.at[d], kc_recv.at[d], other
        )

    for d in range(1, Z):

        @pl.when(z + d < Z)
        def _():
            kz_copy(d).start()

    kc_copy(0).start()
    a2a_start(3)

    for d in range(1, Y):
        py_from(d).wait_recv()

    def pc_copy(cc):
        return rcopy(pg.at[cc], pg.at[cc], pc_send, pc_recv, other)

    pc_copy(c).start()

    for d in range(1, Z):

        @pl.when(z - d >= 0)
        def _():
            kz_from(d).wait_recv()
            kc_copy(d).start()

    a2a_wait(2)
    for g in range(G):
        qr[g * T : (g + 1) * T, :] = q_all[:, g * W : (g + 1) * W]

    pc_copy(1 - c).wait_recv()
    units = []
    for s in range(Y * Z * 2):
        units.append(pg[s % 2, s // (2 * Z), (s // 2) % Z].astype(F32))
    per = KB // U
    for b in range(NPB):
        part = units[b * per : (b + 1) * per]
        kvb[b, 0] = jnp.concatenate([u[:U] for u in part], axis=0).astype(BF)
        kvb[b, 1] = jnp.concatenate([u[U:] for u in part], axis=0).astype(BF)

    kc_copy(0).wait_send()
    kc_from(0).wait_recv()
    for d in range(1, Z):

        @pl.when(z - d >= 0)
        def _():
            kc_from(d).wait_recv()

    nb = NPB + z + 1
    mx[...] = jnp.full_like(mx, NEG)

    def score_body(b, carry):
        keys = kvb[b, 0]
        kvt[b, 0] = keys.T
        kvt[b, 1] = kvb[b, 1].T
        edge = jnp.where(b == nb - 1, c * T, 1 << 20)
        rel = lax.broadcasted_iota(jnp.int32, (KB, T), 0) - lax.broadcasted_iota(jnp.int32, (KB, T), 1)
        seen = jnp.concatenate([rel <= edge] * GC, axis=1)
        for n in range(NC):
            cols = slice(n * CB, (n + 1) * CB)
            s = dot_nt(keys, qr[cols, :])
            s = jnp.where(seen, s, NEG)
            s_scr[b, :, cols] = s
            mx[:, cols] = jnp.maximum(mx[:, cols], jnp.max(s.reshape(KB // 8, 8, CB), axis=0))
        return carry

    lax.fori_loop(0, nb, score_body, 0)
    top = jnp.max(mx[...], axis=0, keepdims=True) * c2
    lx[...] = jnp.zeros_like(lx)
    o_acc[...] = jnp.zeros_like(o_acc)

    def weight_body(b, carry):
        vt = kvt[b, 1]
        for n in range(NC):
            cols = slice(n * CB, (n + 1) * CB)
            e = jnp.exp2(s_scr[b, :, cols] * c2 - top[:, cols])
            lx[:, cols] += jnp.sum(e.reshape(KB // 8, 8, CB), axis=0)
            p = e.astype(BF)
            p_scr[b, :, cols] = p
            o_acc[:, cols] += dot_nn(vt, p)
        return carry

    lax.fori_loop(0, nb, weight_body, 0)
    inv = 1.0 / jnp.sum(lx[...], axis=0, keepdims=True)

    length = len_ref[y]
    first = (2 * z + c) * T
    live_col = first + lax.broadcasted_iota(jnp.int32, (W, T), 1) < length
    live_row = first + lax.broadcasted_iota(jnp.int32, (T, W), 0) < length

    a2a_wait(3)
    deltas = []
    for g in range(G):
        rows = slice(g * T, (g + 1) * T)
        out_t = jnp.where(live_col, o_acc[:, rows] * inv[:, rows], 0.0).astype(BF)
        att_ref[:, g * W : (g + 1) * W] = out_t.T
        grad = jnp.where(live_row, do_all[:, g * W : (g + 1) * W].astype(F32), 0.0)
        dor[rows, :] = grad.astype(BF)
        grad_t = grad.T
        dot_t[:, rows] = grad_t.astype(BF)
        deltas.append(jnp.sum(grad_t * out_t.astype(F32), axis=0, keepdims=True))
    delta = jnp.concatenate(deltas, axis=1)
    dq_acc[...] = jnp.zeros_like(dq_acc)

    def gx_copy(p):
        return rcopy(xs.at[p, 1 - c], xr.at[p], gx_send.at[p], gx_recv.at[p], other)

    def gz_copy(p):
        return rcopy(zs.at[p], zr.at[z - p], gz_send.at[p], gz_recv.at[z - p], at(y, p, c, h))

    def gz_from(d):
        return rcopy(zs.at[z], zr.at[d], gz_send.at[z], gz_recv.at[d], at(y, z + d, c, h))

    def rc_copy():
        return rcopy(prom_s.at[1 - c], prom_r, rc_send, rc_recv, other)

    def ry_copy(d):
        t = (y + d) % Y
        return rcopy(prom_s.at[c, t], prom_y.at[d], ry_send.at[d], ry_recv.at[d], at(t, z, c, h))

    def rz_copy(d):
        t = (z + d) % Z
        return rcopy(prom_y.at[0, t], prom_z.at[d], rz_send.at[d], rz_recv.at[d], at(y, t, c, h))

    def grad_body(b, carry):
        values = kvb[b, 1]
        kt = kvt[b, 0]
        for n in range(NC):
            cols = slice(n * CB, (n + 1) * CB)
            dp = dot_nn(values, dot_t[:, cols])
            w = p_scr[b, :, cols].astype(F32) * inv[:, cols]
            ds = (w * (dp - delta[:, cols])).astype(BF)
            dv = dot_nn(w.astype(BF), dor[cols, :])
            dk = dot_nn(ds, qr[cols, :])
            dq_acc[:, cols] += dot_nn(kt, ds)
            if n == 0:
                acc[0] = dk
                acc[1] = dv
            else:
                acc[0] += dk
                acc[1] += dv

        per_y = Z * 2

        for blk in range(NPB):

            @pl.when(b == blk)
            def _():
                for i in range(KB // U):
                    s = blk * (KB // U) + i
                    rows = slice(i * U, (i + 1) * U)
                    both = jnp.concatenate([acc[0, rows, :] * scale, acc[1, rows, :]], axis=0)
                    prom_s[s % 2, s // per_y, (s // 2) % Z] = both.astype(BF)

        @pl.when(b == NPB - 1)
        def _():
            rc_copy().start()

        @pl.when(b >= NPB)
        def _():
            p = b - NPB
            for half in range(2):
                rows = slice(half * T, (half + 1) * T)
                xs[p, half, 0] = (acc[0, rows, :] * scale).astype(BF)
                xs[p, half, 1] = acc[1, rows, :].astype(BF)
            gx_copy(p).start()

        @pl.when(b == NPB)
        def _():
            rc_copy().wait()
            prom_s[c] = (prom_s[c].astype(F32) + prom_r[...].astype(F32)).astype(BF)
            for d in range(1, Y):
                ry_copy(d).start()

        @pl.when(b > NPB)
        def _():
            p = b - NPB - 1
            gx_copy(p).wait()
            zs[p] = (xs[p, c].astype(F32) + xr[p].astype(F32)).astype(BF)
            gz_copy(p).start()

        return carry

    lax.fori_loop(0, nb, grad_body, 0)

    for g in range(G):
        rows = slice(g * T, (g + 1) * T)
        dq_ref[:, g * W : (g + 1) * W] = (dq_acc[:, rows] * scale).T.astype(BF)

    total = prom_s[c, y].astype(F32)
    for d in range(1, Y):
        ry_copy(d).wait_recv()
        total += prom_y[d].astype(F32)
    prom_y[0] = total.astype(BF)
    for d in range(1, Z):
        rz_copy(d).start()

    gx_copy(z).wait()
    mine = xs[z, c].astype(F32) + xr[z].astype(F32)
    acc2 = acc
    acc2[0, :T] = mine[0]
    acc2[1, :T] = mine[1]
    for d in range(1, Z):

        @pl.when(z + d < Z)
        def _():
            gz_from(d).wait_recv()
            acc2[0, :T] += zr[d, 0].astype(F32)
            acc2[1, :T] += zr[d, 1].astype(F32)

    dkv_ref[0] = acc2[0, :T].astype(BF)
    dkv_ref[1] = acc2[1, :T].astype(BF)

    last = prom_y[0, z].astype(F32)
    for d in range(1, Z):
        rz_copy(d).wait_recv()
        last += prom_z[d].astype(F32)
    prom_ref[...] = last

    for a in range(4):
        for d in range(1, H):
            a2a_copy(a, d).wait_send()
    for d in range(1, Z):
        pz_copy(d).wait_send()
        rz_copy(d).wait_send()
    for d in range(1, Y):
        py_copy(d).wait_send()
        ry_copy(d).wait_send()
    pc_copy(c).wait_send()
    for d in range(1, Z):

        @pl.when(z + d < Z)
        def _():
            kz_copy(d).wait_send()

        @pl.when(z - d >= 0)
        def _():
            kc_copy(d).wait_send()
            gz_copy(z - d).wait_send()


def solution(mesh):
    H = mesh.shape["head"]
    S = mesh.shape["seq"]

    def per_device(q, rk, rv, pk, pv, do, lengths):
        TR = q.shape[0]
        T = TR * H
        Y = lengths.shape[0]
        Z = S // Y // 2
        U = pk.shape[0]
        R = T * G
        NB = U * S // KB + Z
        dims = (H, Y, Z, TR, U)
        dma = pltpu.SemaphoreType.DMA
        vm = pltpu.VMEM
        any_spec = pl.BlockSpec(memory_space=pl.ANY)
        vm_spec = pl.BlockSpec(memory_space=pltpu.VMEM)
        att, dq, dkv, prom = pl.pallas_call(
            functools.partial(kernel, dims),
            out_shape=[
                jax.ShapeDtypeStruct((T, G * W), BF),
                jax.ShapeDtypeStruct((T, G * W), BF),
                jax.ShapeDtypeStruct((2, T, W), BF),
                jax.ShapeDtypeStruct((2 * U, W), F32),
            ],
            in_specs=[
                any_spec,
                any_spec,
                any_spec,
                vm_spec,
                vm_spec,
                any_spec,
                pl.BlockSpec(memory_space=pltpu.SMEM),
            ],
            out_specs=[vm_spec] * 4,
            scratch_shapes=[
                vm((T, G * W), BF),
                vm((T, G * W), BF),
                vm((NB, 2, KB, W), BF),
                vm((NB, 2, W, KB), BF),
                vm((2, Y, Z, 2 * U, W), BF),
                vm((R, W), BF),
                vm((R, W), BF),
                vm((W, R), BF),
                vm((NB, KB, R), F32),
                vm((NB, KB, R), BF),
                vm((8, R), F32),
                vm((8, R), F32),
                vm((W, R), F32),
                vm((W, R), F32),
                vm((2, KB, W), F32),
                vm((2, Y, Z, 2 * U, W), BF),
                vm((Y, Z, 2 * U, W), BF),
                vm((Y, Z, 2 * U, W), BF),
                vm((Z, 2 * U, W), BF),
                vm((Z, 2, 2, T, W), BF),
                vm((Z, 2, T, W), BF),
                vm((Z, 2, T, W), BF),
                vm((Z, 2, T, W), BF),
                dma((4, H)),
                dma((4, H)),
                dma((4,)),
                dma((Z,)),
                dma((Z,)),
                dma((Y,)),
                dma((Y,)),
                dma,
                dma,
                dma((Z,)),
                dma((Z,)),
                dma((Z,)),
                dma((Z,)),
                dma((Z,)),
                dma((Z,)),
                dma((Z,)),
                dma((Z,)),
                dma,
                dma,
                dma((Y,)),
                dma((Y,)),
                dma((Z,)),
                dma((Z,)),
            ],
            compiler_params=pltpu.CompilerParams(
                collective_id=0, has_side_effects=True, vmem_limit_bytes=48 * 1024 * 1024
            ),
        )(q, rk, rv, pk, pv, do, lengths)
        return att, dq, dkv[0], dkv[1], prom[:U], prom[U:]

    tok = P(("seq", "head"), None)
    par = P("seq", "head")
    return jax.shard_map(
        per_device,
        mesh=mesh,
        in_specs=(tok, tok, tok, par, par, tok, P()),
        out_specs=(par,) * 6,
        check_vma=False,
    )
```

time: 903 us -> 58.3 us (0.06)
  waiting for transfers between devices: 565 us -> 0 us
  blocking collectives: 169 us -> 0 us
  starting transfers between devices: 59.1 us -> 0 us
  Pallas kernels: 0 us -> 49.2 us
  local copies, waits for them, and re-layouts: 55.6 us -> 8.06 us
  matrix products: 20 us -> 0 us
  other arithmetic: 16.5 us -> 0 us
  between operations: 15.9 us -> 0.66 us
    unnamed x2 -> x0, waiting for transfers between devices: 550 us -> none
    all_gather x2 -> x0, blocking collectives: 169 us -> none  [the longest x1 88.8 us: per_device(): lax.all_gather(shared_prompt_keys, 'seq', axis=0, tiled=True)]
    pallas_call x0 -> x1, Pallas kernels: none -> 49.2 us  [per_device(): pl.pallas_call(functools.partial(kernel, dims), out_shape=[jax.ShapeDtype...]
    ppermute x14 -> x0, starting transfers between devices: 36.2 us -> none  [from_behind(): return lax.ppermute(block, axis, route)]
    unnamed x155 -> x16, local copies, waits for them, and re-layouts: 30.6 us -> 6.83 us
    all_to_all x4 -> x0, starting transfers between devices: 22.9 us -> none  [the longest x1 6.66 us: per_device(): lax.all_to_all(response_keys, 'head', split_axis=1, concat_axis=0, tiled=...]
    dot_general x60 -> x0, matrix products: 20 us -> none  [the longest x10 6.34 us: per_device(): jnp.einsum('tkgc,ckd->tkgd', weights_bf, block_values, preferred_element_...]
    another operation x10 -> x0, local copies, waits for them, and re-layouts: 19 us -> none
  transfers between devices with their start and end apart: 19 -> 0, of which waited for: 5 -> 0; matrix products, arithmetic and copies ran while one was open for 3% -> 0% of each run, Pallas kernels for 0% -> 0%
where the time goes in v1:
time: 58.3 us; the launch traced here: 57.9 us
  Pallas kernels  49.2 us (84%)
  local copies, waits for them, and re-layouts  8.06 us (14%)
  between operations  0.66 us (1%)
    pallas_call x1, Pallas kernels, per_device(): pl.pallas_call(functools.partial(kernel, dims), out_shape=[jax.ShapeDtype...  49.2 us
    unnamed x16, local copies, waits for them, and re-layouts  6.83 us

profile of v1, /device:TPU:1, one launch (start us, length us, event | category | flops | bytes accessed | tf_op | source)
XLA Modules:
  0.0 57.9 jit_solution(14548789028194869311)
XLA Ops:
  0.6 0.0 copy-start
  0.6 0.9 %copy-done = bf16[16,8192]{1,0:T(8,128)(2,1)S(1)} copy-done((bf16[16,8192]{1,0:T(8,128)(2,1)S(1)}, bf16[16,8192]{1,0:T(8,128)(2,1)}, u32[]{:S(2)}) %copy-start) | copy-done | bytes 262168
  1.6 0.0 copy-start.1
  1.6 0.9 %copy-done.1 = bf16[16,8192]{1,0:T(8,128)(2,1)S(1)} copy-done((bf16[16,8192]{1,0:T(8,128)(2,1)S(1)}, bf16[16,8192]{1,0:T(8,128)(2,1)}, u32[]{:S(2)}) %copy-start.1) | copy-done | bytes 262168
  2.5 0.0 copy-start.2
  2.5 0.8 %copy-done.2 = bf16[16,1024]{1,0:T(8,128)(2,1)S(1)} copy-done((bf16[16,1024]{1,0:T(8,128)(2,1)S(1)}, bf16[16,1024]{1,0:T(8,128)(2,1)}, u32[]{:S(2)}) %copy-start.2) | copy-done | bytes 32792
  3.3 0.0 copy-start.3
  3.3 0.8 %copy-done.3 = bf16[16,1024]{1,0:T(8,128)(2,1)S(1)} copy-done((bf16[16,1024]{1,0:T(8,128)(2,1)S(1)}, bf16[16,1024]{1,0:T(8,128)(2,1)}, u32[]{:S(2)}) %copy-start.3) | copy-done | bytes 32792
  4.1 0.0 copy-start.4
  4.1 0.7 %copy-done.4 = bf16[8,128]{1,0:T(8,128)(2,1)S(1)} copy-done((bf16[8,128]{1,0:T(8,128)(2,1)S(1)}, bf16[8,128]{1,0:T(8,128)(2,1)}, u32[]{:S(2)}) %copy-start.4) | copy-done | bytes 2072
  4.7 0.0 copy-start.5
  4.7 0.7 %copy-done.5 = bf16[8,128]{1,0:T(8,128)(2,1)S(1)} copy-done((bf16[8,128]{1,0:T(8,128)(2,1)S(1)}, bf16[8,128]{1,0:T(8,128)(2,1)}, u32[]{:S(2)}) %copy-start.5) | copy-done | bytes 2072
  5.4 0.0 copy-start.6
  5.4 0.7 %copy-done.6 = s32[8]{0:T(128)S(1)} copy-done((s32[8]{0:T(128)S(1)}, s32[8]{0:T(128)}, u32[]{:S(2)}) %copy-start.6) | copy-done | bytes 56
  6.1 49.2 %shard_map.118 = (bf16[128,1024]{1,0:T(8,128)(2,1)S(1)}, bf16[128,1024]{1,0:T(8,128)(2,1)S(1)}, bf16[2,128,128]{2,1,0:T(8,128)(2,1)S(1)}, f32[16,128]{1,0:T(8,128)S(1)}) custom-call(bf16[16,8192]{1,0:T(8,128)(2,1)S(1)} %copy-done, bf16[16,1024]{1,0:T(8,128)(2,1)S(1)} %copy-done.2, bf16[16,1024]{1,0:T(8,128)(2,1)S(1)} %copy-done.3, ...), custom_call_target="tpu_custom_call" | custom-call | tf_op jit(solution)/shard_map/pallas_call | solution.py:474
  55.3 0.6 %fusion = (f32[8,128]{1,0:T(8,128)}, f32[8,128]{1,0:T(8,128)}) fusion(f32[16,128]{1,0:T(8,128)S(1)} %get-tuple-element.13), kind=kLoop, calls=%fused_computation.2 | loop fusion | bytes 16384 | tf_op jit(solution)/shard_map/slice | solution.py:544
  55.9 0.6 %slice_bitcast_fusion = (bf16[128,128]{1,0:T(8,128)(2,1)}, bf16[128,128]{1,0:T(8,128)(2,1)}) fusion(bf16[2,128,128]{2,1,0:T(8,128)(2,1)S(1)} %get-tuple-element.12), kind=kLoop, calls=%fused_computation | loop fusion | bytes 131072 | tf_op jit(solution)/shard_map/squeeze | solution.py:544
  56.5 0.7 %copy.15 = bf16[128,1024]{1,0:T(8,128)(2,1)} copy(bf16[128,1024]{1,0:T(8,128)(2,1)S(1)} %get-tuple-element.24) | data formatting | bytes 524288
  57.2 0.7 %copy.16 = bf16[128,1024]{1,0:T(8,128)(2,1)} copy(bf16[128,1024]{1,0:T(8,128)(2,1)S(1)} %get-tuple-element.25) | data formatting | bytes 524288
Async XLA Ops:
  0.6 1.0 %copy-start = (bf16[16,8192]{1,0:T(8,128)(2,1)S(1)}, bf16[16,8192]{1,0:T(8,128)(2,1)}, u32[]{:S(2)}) copy-start(bf16[16,8192]{1,0:T(8,128)(2,1)} %q_hbm.1) | copy-start | bytes 786436
  1.6 0.9 %copy-start.1 = (bf16[16,8192]{1,0:T(8,128)(2,1)S(1)}, bf16[16,8192]{1,0:T(8,128)(2,1)}, u32[]{:S(2)}) copy-start(bf16[16,8192]{1,0:T(8,128)(2,1)} %do_hbm.1) | copy-start | bytes 786436
  2.5 0.8 %copy-start.2 = (bf16[16,1024]{1,0:T(8,128)(2,1)S(1)}, bf16[16,1024]{1,0:T(8,128)(2,1)}, u32[]{:S(2)}) copy-start(bf16[16,1024]{1,0:T(8,128)(2,1)} %k_hbm.1) | copy-start | bytes 98308
  3.3 0.8 %copy-start.3 = (bf16[16,1024]{1,0:T(8,128)(2,1)S(1)}, bf16[16,1024]{1,0:T(8,128)(2,1)}, u32[]{:S(2)}) copy-start(bf16[16,1024]{1,0:T(8,128)(2,1)} %v_hbm.1) | copy-start | bytes 98308
  4.1 0.7 %copy-start.4 = (bf16[8,128]{1,0:T(8,128)(2,1)S(1)}, bf16[8,128]{1,0:T(8,128)(2,1)}, u32[]{:S(2)}) copy-start(bf16[8,128]{1,0:T(8,128)(2,1)} %pk_ref.1) | copy-start | bytes 6148
  4.7 0.7 %copy-start.5 = (bf16[8,128]{1,0:T(8,128)(2,1)S(1)}, bf16[8,128]{1,0:T(8,128)(2,1)}, u32[]{:S(2)}) copy-start(bf16[8,128]{1,0:T(8,128)(2,1)} %pv_ref.1) | copy-start | bytes 6148
  5.4 0.7 %copy-start.6 = (s32[8]{0:T(128)S(1)}, s32[8]{0:T(128)}, u32[]{:S(2)}) copy-start(s32[8]{0:T(128)} %len_ref.1) | copy-start | bytes 100

commit v2 on v1

--- a/solution.py
+++ b/solution.py
@@ -31,14 +31,27 @@
     q_hbm,
     k_hbm,
     v_hbm,
+    pk_hbm,
+    pv_hbm,
+    do_hbm,
+    len_hbm,
+    att_ref,
+    dq_ref,
+    dk_ref,
+    dv_ref,
+    pdk_ref,
+    pdv_ref,
     pk_ref,
     pv_ref,
-    do_hbm,
     len_ref,
-    att_ref,
-    dq_ref,
-    dkv_ref,
-    prom_ref,
+    small_sem,
+    out_sem,
+    att_v,
+    dq_v,
+    dk_v,
+    dv_v,
+    pdk_v,
+    pdv_v,
     q_all,
     do_all,
     kvb,
@@ -112,8 +125,13 @@
 
     other = at(y, z, 1 - c, h)
 
-    unit = jnp.concatenate([pk_ref[...].astype(F32), pv_ref[...].astype(F32)], axis=0)
-    pg[c, y, z] = unit.astype(BF)
+    small = [
+        pltpu.make_async_copy(pk_hbm, pk_ref, small_sem.at[0]),
+        pltpu.make_async_copy(pv_hbm, pv_ref, small_sem.at[1]),
+        pltpu.make_async_copy(len_hbm, len_ref, small_sem.at[2]),
+    ]
+    for copy in small:
+        copy.start()
 
     barrier = pltpu.get_barrier_semaphore()
     for d in range(1, H):
@@ -166,6 +184,11 @@
     a2a_start(0)
     a2a_start(1)
 
+    for copy in small:
+        copy.wait()
+    unit = jnp.concatenate([pk_ref[...].astype(F32), pv_ref[...].astype(F32)], axis=0)
+    pg[c, y, z] = unit.astype(BF)
+
     def pz_copy(d):
         return rcopy(
             pg.at[c, y, z], pg.at[c, y, z], pz_send.at[d], pz_recv.at[d], at(y, (z + d) % Z, c, h)
@@ -178,8 +201,6 @@
     for d in range(1, Z):
         pz_copy(d).start()
     a2a_start(2)
-    for d in range(1, Z):
-        pz_from(d).wait_recv()
 
     def py_copy(d):
         return rcopy(pg.at[c, y], pg.at[c, y], py_send.at[d], py_recv.at[d], at((y + d) % Y, z, c, h))
@@ -187,12 +208,6 @@
     def py_from(d):
         f = (y + Y - d) % Y
         return rcopy(pg.at[c, f], pg.at[c, f], py_send.at[d], py_recv.at[d], at(f, z, c, h))
-
-    for d in range(1, Y):
-        py_copy(d).start()
-
-    a2a_wait(0)
-    a2a_wait(1)
 
     def span_ref(zz, cc):
         return kvb.at[NPB + zz, :, pl.ds(pl.multiple_of(cc * T, T), T), :]
@@ -215,56 +230,28 @@
             span_ref(z - d, 1 - c), span_ref(z - d, 1 - c), kc_send.at[d], kc_recv.at[d], other
         )
 
-    for d in range(1, Z):
-
-        @pl.when(z + d < Z)
-        def _():
-            kz_copy(d).start()
-
-    kc_copy(0).start()
-    a2a_start(3)
-
-    for d in range(1, Y):
-        py_from(d).wait_recv()
-
     def pc_copy(cc):
         return rcopy(pg.at[cc], pg.at[cc], pc_send, pc_recv, other)
 
-    pc_copy(c).start()
-
-    for d in range(1, Z):
-
-        @pl.when(z - d >= 0)
-        def _():
-            kz_from(d).wait_recv()
-            kc_copy(d).start()
-
-    a2a_wait(2)
-    for g in range(G):
-        qr[g * T : (g + 1) * T, :] = q_all[:, g * W : (g + 1) * W]
-
-    pc_copy(1 - c).wait_recv()
-    units = []
-    for s in range(Y * Z * 2):
-        units.append(pg[s % 2, s // (2 * Z), (s // 2) % Z].astype(F32))
-    per = KB // U
-    for b in range(NPB):
-        part = units[b * per : (b + 1) * per]
-        kvb[b, 0] = jnp.concatenate([u[:U] for u in part], axis=0).astype(BF)
-        kvb[b, 1] = jnp.concatenate([u[U:] for u in part], axis=0).astype(BF)
-
-    kc_copy(0).wait_send()
-    kc_from(0).wait_recv()
-    for d in range(1, Z):
-
-        @pl.when(z - d >= 0)
-        def _():
-            kc_from(d).wait_recv()
+    a2a_wait(0)
+    a2a_wait(1)
+    for d in range(1, Z):
+
+        @pl.when(z + d < Z)
+        def _():
+            kz_copy(d).start()
+
+    kc_copy(0).start()
+    for d in range(1, Z):
+        pz_from(d).wait_recv()
+    for d in range(1, Y):
+        py_copy(d).start()
+    a2a_start(3)
 
     nb = NPB + z + 1
     mx[...] = jnp.full_like(mx, NEG)
 
-    def score_body(b, carry):
+    def scores(b):
         keys = kvb[b, 0]
         kvt[b, 0] = keys.T
         kvt[b, 1] = kvb[b, 1].T
@@ -277,6 +264,40 @@
             s = jnp.where(seen, s, NEG)
             s_scr[b, :, cols] = s
             mx[:, cols] = jnp.maximum(mx[:, cols], jnp.max(s.reshape(KB // 8, 8, CB), axis=0))
+
+    a2a_wait(2)
+    for g in range(G):
+        qr[g * T : (g + 1) * T, :] = q_all[:, g * W : (g + 1) * W]
+    for d in range(1, Y):
+        py_from(d).wait_recv()
+    pc_copy(c).start()
+    for d in range(1, Z):
+
+        @pl.when(z - d >= 0)
+        def _():
+            kz_from(d).wait_recv()
+            kc_copy(d).start()
+
+    pc_copy(1 - c).wait_recv()
+    units = []
+    for s in range(Y * Z * 2):
+        units.append(pg[s % 2, s // (2 * Z), (s // 2) % Z].astype(F32))
+    per = KB // U
+    for b in range(NPB):
+        part = units[b * per : (b + 1) * per]
+        kvb[b, 0] = jnp.concatenate([u[:U] for u in part], axis=0).astype(BF)
+        kvb[b, 1] = jnp.concatenate([u[U:] for u in part], axis=0).astype(BF)
+
+    kc_copy(0).wait_send()
+    kc_from(0).wait_recv()
+    for d in range(1, Z):
+
+        @pl.when(z - d >= 0)
+        def _():
+            kc_from(d).wait_recv()
+
+    def score_body(b, carry):
+        scores(b)
         return carry
 
     lax.fori_loop(0, nb, score_body, 0)
@@ -303,17 +324,23 @@
     live_col = first + lax.broadcasted_iota(jnp.int32, (W, T), 1) < length
     live_row = first + lax.broadcasted_iota(jnp.int32, (T, W), 0) < length
 
+    for g in range(G):
+        rows = slice(g * T, (g + 1) * T)
+        out_t = jnp.where(live_col, o_acc[:, rows] * inv[:, rows], 0.0)
+        att_v[:, g * W : (g + 1) * W] = out_t.T.astype(BF)
+        o_acc[:, rows] = out_t.astype(BF).astype(F32)
+    att_out = pltpu.make_async_copy(att_v, att_ref, out_sem.at[0])
+    att_out.start()
+
     a2a_wait(3)
     deltas = []
     for g in range(G):
         rows = slice(g * T, (g + 1) * T)
-        out_t = jnp.where(live_col, o_acc[:, rows] * inv[:, rows], 0.0).astype(BF)
-        att_ref[:, g * W : (g + 1) * W] = out_t.T
         grad = jnp.where(live_row, do_all[:, g * W : (g + 1) * W].astype(F32), 0.0)
         dor[rows, :] = grad.astype(BF)
         grad_t = grad.T
         dot_t[:, rows] = grad_t.astype(BF)
-        deltas.append(jnp.sum(grad_t * out_t.astype(F32), axis=0, keepdims=True))
+        deltas.append(jnp.sum(grad_t * o_acc[:, rows], axis=0, keepdims=True))
     delta = jnp.concatenate(deltas, axis=1)
     dq_acc[...] = jnp.zeros_like(dq_acc)
 
@@ -400,7 +427,9 @@
 
     for g in range(G):
         rows = slice(g * T, (g + 1) * T)
-        dq_ref[:, g * W : (g + 1) * W] = (dq_acc[:, rows] * scale).T.astype(BF)
+        dq_v[:, g * W : (g + 1) * W] = (dq_acc[:, rows] * scale).T.astype(BF)
+    dq_out = pltpu.make_async_copy(dq_v, dq_ref, out_sem.at[1])
+    dq_out.start()
 
     total = prom_s[c, y].astype(F32)
     for d in range(1, Y):
@@ -423,14 +452,25 @@
             acc2[0, :T] += zr[d, 0].astype(F32)
             acc2[1, :T] += zr[d, 1].astype(F32)
 
-    dkv_ref[0] = acc2[0, :T].astype(BF)
-    dkv_ref[1] = acc2[1, :T].astype(BF)
+    dk_v[...] = acc2[0, :T].astype(BF)
+    dv_v[...] = acc2[1, :T].astype(BF)
+    dk_out = pltpu.make_async_copy(dk_v, dk_ref, out_sem.at[2])
+    dv_out = pltpu.make_async_copy(dv_v, dv_ref, out_sem.at[3])
+    dk_out.start()
+    dv_out.start()
 
     last = prom_y[0, z].astype(F32)
     for d in range(1, Z):
         rz_copy(d).wait_recv()
         last += prom_z[d].astype(F32)
-    prom_ref[...] = last
+    pdk_v[...] = last[:U]
+    pdv_v[...] = last[U:]
+    pdk_out = pltpu.make_async_copy(pdk_v, pdk_ref, out_sem.at[4])
+    pdv_out = pltpu.make_async_copy(pdv_v, pdv_ref, out_sem.at[5])
+    pdk_out.start()
+    pdv_out.start()
+    for copy in (att_out, dq_out, dk_out, dv_out, pdk_out, pdv_out):
+        copy.wait()
 
     for a in range(4):
         for d in range(1, H):
@@ -452,6 +492,19 @@
         def _():
             kc_copy(d).wait_send()
             gz_copy(z - d).wait_send()
+
+
+def write_out(*refs):
+    given, written, held, sems = refs[:6], refs[6:12], refs[12:18], refs[18]
+    reads = [pltpu.make_async_copy(given[i], held[i], sems.at[0, i]) for i in range(6)]
+    writes = [pltpu.make_async_copy(held[i], written[i], sems.at[1, i]) for i in range(6)]
+    for copy in reads:
+        copy.start()
+    for i in range(6):
+        reads[i].wait()
+        writes[i].start()
+    for copy in writes:
+        copy.wait()
 
 
 def solution(mesh):
@@ -470,26 +523,28 @@
         dma = pltpu.SemaphoreType.DMA
         vm = pltpu.VMEM
         any_spec = pl.BlockSpec(memory_space=pl.ANY)
-        vm_spec = pl.BlockSpec(memory_space=pltpu.VMEM)
-        att, dq, dkv, prom = pl.pallas_call(
+        shapes = [
+            jax.ShapeDtypeStruct((T, G * W), BF),
+            jax.ShapeDtypeStruct((T, G * W), BF),
+            jax.ShapeDtypeStruct((T, W), BF),
+            jax.ShapeDtypeStruct((T, W), BF),
+            jax.ShapeDtypeStruct((U, W), F32),
+            jax.ShapeDtypeStruct((U, W), F32),
+        ]
+        results = pl.pallas_call(
             functools.partial(kernel, dims),
-            out_shape=[
-                jax.ShapeDtypeStruct((T, G * W), BF),
-                jax.ShapeDtypeStruct((T, G * W), BF),
-                jax.ShapeDtypeStruct((2, T, W), BF),
-                jax.ShapeDtypeStruct((2 * U, W), F32),
-            ],
-            in_specs=[
-                any_spec,
-                any_spec,
-                any_spec,
-                vm_spec,
-                vm_spec,
-                any_spec,
-                pl.BlockSpec(memory_space=pltpu.SMEM),
-            ],
-            out_specs=[vm_spec] * 4,
+            out_shape=shapes,
+            in_specs=[any_spec] * 7,
+            out_specs=[any_spec] * 6,
             scratch_shapes=[
+                vm((U, W), BF),
+                vm((U, W), BF),
+                pltpu.SMEM((Y,), jnp.int32),
+                dma((3,)),
+                dma((6,)),
+            ]
+            + [vm(x.shape, x.dtype) for x in shapes]
+            + [
                 vm((T, G * W), BF),
                 vm((T, G * W), BF),
                 vm((NB, 2, KB, W), BF),
@@ -538,10 +593,17 @@
                 dma((Z,)),
             ],
             compiler_params=pltpu.CompilerParams(
-                collective_id=0, has_side_effects=True, vmem_limit_bytes=48 * 1024 * 1024
+                collective_id=0, has_side_effects=True, vmem_limit_bytes=60 * 1024 * 1024
             ),
         )(q, rk, rv, pk, pv, do, lengths)
-        return att, dq, dkv[0], dkv[1], prom[:U], prom[U:]
+        return pl.pallas_call(
+            write_out,
+            out_shape=shapes,
+            in_specs=[any_spec] * 6,
+            out_specs=[any_spec] * 6,
+            scratch_shapes=[vm(x.shape, x.dtype) for x in shapes] + [dma((2, 6))],
+            compiler_params=pltpu.CompilerParams(vmem_limit_bytes=60 * 1024 * 1024),
+        )(*results)
 
     tok = P(("seq", "head"), None)
     par = P("seq", "head")

time: 58.3 us -> 51.9 us (0.89)
  local copies, waits for them, and re-layouts: 8.06 us -> 0 us
  Pallas kernels: 49.2 us -> 50.6 us
    unnamed x16 -> x0, local copies, waits for them, and re-layouts: 6.83 us -> none
    pallas_call x1 -> x2, Pallas kernels: 49.2 us -> 50.6 us  [the longest x1 48.7 us: per_device(): pl.pallas_call(functools.partial(kernel, dims), out_shape=shapes, in_spec...]
    squeeze x1 -> x0, local copies, waits for them, and re-layouts: 0.63 us -> none  [per_device(): return (att, dq, dkv[0], dkv[1], prom[:U], prom[U:])]
    slice x1 -> x0, local copies, waits for them, and re-layouts: 0.6 us -> none  [per_device(): return (att, dq, dkv[0], dkv[1], prom[:U], prom[U:])]
where the time goes in v2:
time: 51.9 us; the launch traced here: 51.2 us
  Pallas kernels  50.6 us (97%)
  between operations  0.64 us (1%)
    pallas_call x1, Pallas kernels, per_device(): pl.pallas_call(functools.partial(kernel, dims), out_shape=shapes, in_spec...  48.7 us
    pallas_call x1, Pallas kernels, per_device(): pl.pallas_call(write_out, out_shape=shapes, in_specs=[any_spec] * 6, out_...  1.86 us

profile of v2, /device:TPU:1, one launch (start us, length us, event | category | flops | bytes accessed | tf_op | source)
XLA Modules:
  0.0 51.2 jit_solution(7594398138895448927)
XLA Ops:
  0.6 48.7 %shard_map.118 = (bf16[128,1024]{1,0:T(8,128)(2,1)}, bf16[128,1024]{1,0:T(8,128)(2,1)}, bf16[128,128]{1,0:T(8,128)(2,1)}, bf16[128,128]{1,0:T(8,128)(2,1)}, f32[8,128]{1,0:T(8,128)}, /*index=5*/f32[8,128]{1,0:T(8,128)}) custom-call(bf16[16,8192]{1,0:T(8,128)(2,1)} %q_hbm.1, bf16[16,1024]{1,0:T(8,128)(2,1)} %k_hbm.1, bf16[16,1024]{1,0:T(8,128)(2,1)} %v_hbm.1, ...), custom_call_target="tpu_custom_call" | custom-call | tf_op jit(solution)/shard_map/pallas_call | solution.py:534
  49.3 1.9 %shard_map.119 = (bf16[128,1024]{1,0:T(8,128)(2,1)}, bf16[128,1024]{1,0:T(8,128)(2,1)}, bf16[128,128]{1,0:T(8,128)(2,1)}, bf16[128,128]{1,0:T(8,128)(2,1)}, f32[8,128]{1,0:T(8,128)}, /*index=5*/f32[8,128]{1,0:T(8,128)}) custom-call(bf16[128,1024]{1,0:T(8,128)(2,1)} %get-tuple-element.12.refs_0_, bf16[128,1024]{1,0:T(8,128)(2,1)} %get-tuple-element.13.refs_1_, ...), custom_call_target="tpu_custom_call" | custom-call | tf_op jit(solution)/shard_map/pallas_call | solution.py:599

commit v3 on v2

--- a/solution.py
+++ b/solution.py
@@ -14,7 +14,7 @@
 W = 128
 G = 8
 KB = 256
-CB = 256
+CB = 512
 NEG = -1e30
 
 
@@ -44,6 +44,7 @@
     pk_ref,
     pv_ref,
     len_ref,
+    kv_held,
     small_sem,
     out_sem,
     att_v,
@@ -129,6 +130,8 @@
         pltpu.make_async_copy(pk_hbm, pk_ref, small_sem.at[0]),
         pltpu.make_async_copy(pv_hbm, pv_ref, small_sem.at[1]),
         pltpu.make_async_copy(len_hbm, len_ref, small_sem.at[2]),
+        pltpu.make_async_copy(k_hbm, kv_held.at[0], small_sem.at[3]),
+        pltpu.make_async_copy(v_hbm, kv_held.at[1], small_sem.at[4]),
     ]
     for copy in small:
         copy.start()
@@ -153,10 +156,8 @@
         wide = pl.ds(pl.multiple_of(t * GW, GW), GW)
         thin = pl.ds(pl.multiple_of(t * W, W), W)
         if a == 0:
-            return k_hbm.at[:, thin], kvb.at[my_blk, 0, kv_row, :]
+            return kv_held.at[:, :, thin], kvb.at[my_blk, :, kv_row, :]
         if a == 1:
-            return v_hbm.at[:, thin], kvb.at[my_blk, 1, kv_row, :]
-        if a == 2:
             return q_hbm.at[:, wide], q_all.at[row, :]
         return do_hbm.at[:, wide], do_all.at[row, :]
 
@@ -181,11 +182,10 @@
             src, dst = src_dst(a, h, frm)
             rcopy(src, dst, a2a_send.at[a, d], a2a_recv.at[a, d], at(y, z, c, frm)).wait_recv()
 
-    a2a_start(0)
-    a2a_start(1)
-
     for copy in small:
         copy.wait()
+    a2a_start(0)
+
     unit = jnp.concatenate([pk_ref[...].astype(F32), pv_ref[...].astype(F32)], axis=0)
     pg[c, y, z] = unit.astype(BF)
 
@@ -200,7 +200,7 @@
 
     for d in range(1, Z):
         pz_copy(d).start()
-    a2a_start(2)
+    a2a_start(1)
 
     def py_copy(d):
         return rcopy(pg.at[c, y], pg.at[c, y], py_send.at[d], py_recv.at[d], at((y + d) % Y, z, c, h))
@@ -234,7 +234,6 @@
         return rcopy(pg.at[cc], pg.at[cc], pc_send, pc_recv, other)
 
     a2a_wait(0)
-    a2a_wait(1)
     for d in range(1, Z):
 
         @pl.when(z + d < Z)
@@ -246,26 +245,30 @@
         pz_from(d).wait_recv()
     for d in range(1, Y):
         py_copy(d).start()
-    a2a_start(3)
+    a2a_start(2)
 
     nb = NPB + z + 1
     mx[...] = jnp.full_like(mx, NEG)
 
-    def scores(b):
+    def scores(b, edge):
+        rel = lax.broadcasted_iota(jnp.int32, (KB, T), 0) - lax.broadcasted_iota(jnp.int32, (KB, T), 1)
+        seen = jnp.concatenate([rel <= c * T] * GC, axis=1)
         keys = kvb[b, 0]
         kvt[b, 0] = keys.T
         kvt[b, 1] = kvb[b, 1].T
-        edge = jnp.where(b == nb - 1, c * T, 1 << 20)
-        rel = lax.broadcasted_iota(jnp.int32, (KB, T), 0) - lax.broadcasted_iota(jnp.int32, (KB, T), 1)
-        seen = jnp.concatenate([rel <= edge] * GC, axis=1)
         for n in range(NC):
             cols = slice(n * CB, (n + 1) * CB)
             s = dot_nt(keys, qr[cols, :])
-            s = jnp.where(seen, s, NEG)
+            if edge:
+                s = jnp.where(seen, s, NEG)
             s_scr[b, :, cols] = s
             mx[:, cols] = jnp.maximum(mx[:, cols], jnp.max(s.reshape(KB // 8, 8, CB), axis=0))
 
-    a2a_wait(2)
+    def score_body(b, carry):
+        scores(b, False)
+        return carry
+
+    a2a_wait(1)
     for g in range(G):
         qr[g * T : (g + 1) * T, :] = q_all[:, g * W : (g + 1) * W]
     for d in range(1, Y):
@@ -290,17 +293,15 @@
 
     kc_copy(0).wait_send()
     kc_from(0).wait_recv()
+    scores(nb - 1, True)
+    lax.fori_loop(0, NPB, score_body, 0)
     for d in range(1, Z):
 
         @pl.when(z - d >= 0)
         def _():
             kc_from(d).wait_recv()
 
-    def score_body(b, carry):
-        scores(b)
-        return carry
-
-    lax.fori_loop(0, nb, score_body, 0)
+    lax.fori_loop(NPB, nb - 1, score_body, 0)
     top = jnp.max(mx[...], axis=0, keepdims=True) * c2
     lx[...] = jnp.zeros_like(lx)
     o_acc[...] = jnp.zeros_like(o_acc)
@@ -332,7 +333,7 @@
     att_out = pltpu.make_async_copy(att_v, att_ref, out_sem.at[0])
     att_out.start()
 
-    a2a_wait(3)
+    a2a_wait(2)
     deltas = []
     for g in range(G):
         rows = slice(g * T, (g + 1) * T)
@@ -472,7 +473,7 @@
     for copy in (att_out, dq_out, dk_out, dv_out, pdk_out, pdv_out):
         copy.wait()
 
-    for a in range(4):
+    for a in range(3):
         for d in range(1, H):
             a2a_copy(a, d).wait_send()
     for d in range(1, Z):
@@ -540,7 +541,8 @@
                 vm((U, W), BF),
                 vm((U, W), BF),
                 pltpu.SMEM((Y,), jnp.int32),
-                dma((3,)),
+                vm((2, TR, H * W), BF),
+                dma((5,)),
                 dma((6,)),
             ]
             + [vm(x.shape, x.dtype) for x in shapes]
@@ -568,9 +570,9 @@
                 vm((Z, 2, T, W), BF),
                 vm((Z, 2, T, W), BF),
                 vm((Z, 2, T, W), BF),
-                dma((4, H)),
-                dma((4, H)),
-                dma((4,)),
+                dma((3, H)),
+                dma((3, H)),
+                dma((3,)),
                 dma((Z,)),
                 dma((Z,)),
                 dma((Y,)),

time: 51.9 us -> 49.7 us (0.958)
  Pallas kernels: 50.6 us -> 48.4 us
    pallas_call x1, Pallas kernels: 48.7 us -> 46.5 us  [per_device(): pl.pallas_call(functools.partial(kernel, dims), out_shape=shapes, in_spec...]
where the time goes in v3:
time: 49.7 us; the launch traced here: 49 us
  Pallas kernels  48.4 us (97%)
  between operations  0.64 us (1%)
    pallas_call x1, Pallas kernels, per_device(): pl.pallas_call(functools.partial(kernel, dims), out_shape=shapes, in_spec...  46.5 us
    pallas_call x1, Pallas kernels, per_device(): pl.pallas_call(write_out, out_shape=shapes, in_specs=[any_spec] * 6, out_...  1.86 us

profile of v3, /device:TPU:1, one launch (start us, length us, event | category | flops | bytes accessed | tf_op | source)
XLA Modules:
  0.0 49.0 jit_solution(10092069205715968464)
XLA Ops:
  0.6 46.5 %shard_map.118 = (bf16[128,1024]{1,0:T(8,128)(2,1)}, bf16[128,1024]{1,0:T(8,128)(2,1)}, bf16[128,128]{1,0:T(8,128)(2,1)}, bf16[128,128]{1,0:T(8,128)(2,1)}, f32[8,128]{1,0:T(8,128)}, /*index=5*/f32[8,128]{1,0:T(8,128)}) custom-call(bf16[16,8192]{1,0:T(8,128)(2,1)} %q_hbm.1, bf16[16,1024]{1,0:T(8,128)(2,1)} %k_hbm.1, bf16[16,1024]{1,0:T(8,128)(2,1)} %v_hbm.1, ...), custom_call_target="tpu_custom_call" | custom-call | tf_op jit(solution)/shard_map/pallas_call | solution.py:535
  47.2 1.9 %shard_map.119 = (bf16[128,1024]{1,0:T(8,128)(2,1)}, bf16[128,1024]{1,0:T(8,128)(2,1)}, bf16[128,128]{1,0:T(8,128)(2,1)}, bf16[128,128]{1,0:T(8,128)(2,1)}, f32[8,128]{1,0:T(8,128)}, /*index=5*/f32[8,128]{1,0:T(8,128)}) custom-call(bf16[128,1024]{1,0:T(8,128)(2,1)} %get-tuple-element.12.refs_0_, bf16[128,1024]{1,0:T(8,128)(2,1)} %get-tuple-element.13.refs_1_, ...), custom_call_target="tpu_custom_call" | custom-call | tf_op jit(solution)/shard_map/pallas_call | solution.py:601

commit v4 on v3

--- a/solution.py
+++ b/solution.py
@@ -354,8 +354,11 @@
     def gz_from(d):
         return rcopy(zs.at[z], zr.at[d], gz_send.at[z], gz_recv.at[d], at(y, z + d, c, h))
 
-    def rc_copy():
-        return rcopy(prom_s.at[1 - c], prom_r, rc_send, rc_recv, other)
+    YB = Y // NPB
+
+    def rc_copy(k):
+        ys = pl.ds(k * YB, YB)
+        return rcopy(prom_s.at[1 - c, ys], prom_r.at[ys], rc_send.at[k], rc_recv.at[k], other)
 
     def ry_copy(d):
         t = (y + d) % Y
@@ -395,9 +398,9 @@
                     both = jnp.concatenate([acc[0, rows, :] * scale, acc[1, rows, :]], axis=0)
                     prom_s[s % 2, s // per_y, (s // 2) % Z] = both.astype(BF)
 
-        @pl.when(b == NPB - 1)
-        def _():
-            rc_copy().start()
+            @pl.when(b == blk)
+            def _():
+                rc_copy(blk).start()
 
         @pl.when(b >= NPB)
         def _():
@@ -408,12 +411,19 @@
                 xs[p, half, 1] = acc[1, rows, :].astype(BF)
             gx_copy(p).start()
 
-        @pl.when(b == NPB)
-        def _():
-            rc_copy().wait()
-            prom_s[c] = (prom_s[c].astype(F32) + prom_r[...].astype(F32)).astype(BF)
-            for d in range(1, Y):
-                ry_copy(d).start()
+        for k in range(NPB):
+
+            @pl.when(b == k + 1)
+            def _():
+                rc_copy(k).wait()
+                ys = slice(k * YB, (k + 1) * YB)
+                prom_s[c, ys] = (prom_s[c, ys].astype(F32) + prom_r[ys].astype(F32)).astype(BF)
+                for d in range(1, Y):
+                    t = (y + d) % Y
+
+                    @pl.when(t // YB == k)
+                    def _():
+                        ry_copy(d).start()
 
         @pl.when(b > NPB)
         def _():
@@ -425,20 +435,20 @@
         return carry
 
     lax.fori_loop(0, nb, grad_body, 0)
+
+    total = prom_s[c, y].astype(F32)
+    for d in range(1, Y):
+        ry_copy(d).wait_recv()
+        total += prom_y[d].astype(F32)
+    prom_y[0] = total.astype(BF)
+    for d in range(1, Z):
+        rz_copy(d).start()
 
     for g in range(G):
         rows = slice(g * T, (g + 1) * T)
         dq_v[:, g * W : (g + 1) * W] = (dq_acc[:, rows] * scale).T.astype(BF)
     dq_out = pltpu.make_async_copy(dq_v, dq_ref, out_sem.at[1])
     dq_out.start()
-
-    total = prom_s[c, y].astype(F32)
-    for d in range(1, Y):
-        ry_copy(d).wait_recv()
-        total += prom_y[d].astype(F32)
-    prom_y[0] = total.astype(BF)
-    for d in range(1, Z):
-        rz_copy(d).start()
 
     gx_copy(z).wait()
     mine = xs[z, c].astype(F32) + xr[z].astype(F32)
@@ -587,8 +597,8 @@
                 dma((Z,)),
                 dma((Z,)),
                 dma((Z,)),
-                dma,
-                dma,
+                dma((U * S // KB,)),
+                dma((U * S // KB,)),
                 dma((Y,)),
                 dma((Y,)),
                 dma((Z,)),

time: 49.7 us -> 47.6 us (0.958)
  the two profiles are of different devices: /device:TPU:1 before, /device:TPU:8 now
where the time goes in v4:
time: 47.6 us; the launch traced here: 47.5 us
  Pallas kernels  46.8 us (98%)
  between operations  0.64 us (1%)
    pallas_call x1, Pallas kernels, per_device(): pl.pallas_call(functools.partial(kernel, dims), out_shape=shapes, in_spec...  45 us
    pallas_call x1, Pallas kernels, per_device(): pl.pallas_call(write_out, out_shape=shapes, in_specs=[any_spec] * 6, out_...  1.86 us

profile of v4, /device:TPU:8, one launch (start us, length us, event | category | flops | bytes accessed | tf_op | source)
XLA Modules:
  0.0 47.5 jit_solution(3920909414870022203)
XLA Ops:
  0.6 45.0 %shard_map.118 = (bf16[128,1024]{1,0:T(8,128)(2,1)}, bf16[128,1024]{1,0:T(8,128)(2,1)}, bf16[128,128]{1,0:T(8,128)(2,1)}, bf16[128,128]{1,0:T(8,128)(2,1)}, f32[8,128]{1,0:T(8,128)}, /*index=5*/f32[8,128]{1,0:T(8,128)}) custom-call(bf16[16,8192]{1,0:T(8,128)(2,1)} %q_hbm.1, bf16[16,1024]{1,0:T(8,128)(2,1)} %k_hbm.1, bf16[16,1024]{1,0:T(8,128)(2,1)} %v_hbm.1, ...), custom_call_target="tpu_custom_call" | custom-call | tf_op jit(solution)/shard_map/pallas_call | solution.py:545
  45.6 1.9 %shard_map.119 = (bf16[128,1024]{1,0:T(8,128)(2,1)}, bf16[128,1024]{1,0:T(8,128)(2,1)}, bf16[128,128]{1,0:T(8,128)(2,1)}, bf16[128,128]{1,0:T(8,128)(2,1)}, f32[8,128]{1,0:T(8,128)}, /*index=5*/f32[8,128]{1,0:T(8,128)}) custom-call(bf16[128,1024]{1,0:T(8,128)(2,1)} %get-tuple-element.12.refs_0_, bf16[128,1024]{1,0:T(8,128)(2,1)} %get-tuple-element.13.refs_1_, ...), custom_call_target="tpu_custom_call" | custom-call | tf_op jit(solution)/shard_map/pallas_call | solution.py:611

commit v5 on v4

--- a/solution.py
+++ b/solution.py
@@ -184,8 +184,6 @@
 
     for copy in small:
         copy.wait()
-    a2a_start(0)
-
     unit = jnp.concatenate([pk_ref[...].astype(F32), pv_ref[...].astype(F32)], axis=0)
     pg[c, y, z] = unit.astype(BF)
 
@@ -200,6 +198,7 @@
 
     for d in range(1, Z):
         pz_copy(d).start()
+    a2a_start(0)
     a2a_start(1)
 
     def py_copy(d):
@@ -234,7 +233,7 @@
         return rcopy(pg.at[cc], pg.at[cc], pc_send, pc_recv, other)
 
     a2a_wait(0)
-    for d in range(1, Z):
+    for d in range(Z - 1, 0, -1):
 
         @pl.when(z + d < Z)
         def _():

time: 47.6 us -> 47 us (0.987)
  the two profiles are of different devices: /device:TPU:8 before, /device:TPU:1 now
where the time goes in v5:
time: 47 us; the launch traced here: 46.1 us
  Pallas kernels  45.4 us (97%)
  between operations  0.64 us (1%)
    pallas_call x1, Pallas kernels, per_device(): pl.pallas_call(functools.partial(kernel, dims), out_shape=shapes, in_spec...  43.6 us
    pallas_call x1, Pallas kernels, per_device(): pl.pallas_call(write_out, out_shape=shapes, in_specs=[any_spec] * 6, out_...  1.86 us

profile of v5, /device:TPU:1, one launch (start us, length us, event | category | flops | bytes accessed | tf_op | source)
XLA Modules:
  0.0 46.1 jit_solution(6679523094163491383)
XLA Ops:
  0.6 43.6 %shard_map.118 = (bf16[128,1024]{1,0:T(8,128)(2,1)}, bf16[128,1024]{1,0:T(8,128)(2,1)}, bf16[128,128]{1,0:T(8,128)(2,1)}, bf16[128,128]{1,0:T(8,128)(2,1)}, f32[8,128]{1,0:T(8,128)}, /*index=5*/f32[8,128]{1,0:T(8,128)}) custom-call(bf16[16,8192]{1,0:T(8,128)(2,1)} %q_hbm.1, bf16[16,1024]{1,0:T(8,128)(2,1)} %k_hbm.1, bf16[16,1024]{1,0:T(8,128)(2,1)} %v_hbm.1, ...), custom_call_target="tpu_custom_call" | custom-call | tf_op jit(solution)/shard_map/pallas_call | solution.py:544
  44.2 1.9 %shard_map.119 = (bf16[128,1024]{1,0:T(8,128)(2,1)}, bf16[128,1024]{1,0:T(8,128)(2,1)}, bf16[128,128]{1,0:T(8,128)(2,1)}, bf16[128,128]{1,0:T(8,128)(2,1)}, f32[8,128]{1,0:T(8,128)}, /*index=5*/f32[8,128]{1,0:T(8,128)}) custom-call(bf16[128,1024]{1,0:T(8,128)(2,1)} %get-tuple-element.12.refs_0_, bf16[128,1024]{1,0:T(8,128)(2,1)} %get-tuple-element.13.refs_1_, ...), custom_call_target="tpu_custom_call" | custom-call | tf_op jit(solution)/shard_map/pallas_call | solution.py:610

commit v6 on v5

--- a/solution.py
+++ b/solution.py
@@ -367,6 +367,11 @@
         t = (z + d) % Z
         return rcopy(prom_y.at[0, t], prom_z.at[d], rz_send.at[d], rz_recv.at[d], at(y, t, c, h))
 
+    def pass_on(p):
+        gx_copy(p).wait()
+        zs[p] = (xs[p, c].astype(F32) + xr[p].astype(F32)).astype(BF)
+        gz_copy(p).start()
+
     def grad_body(b, carry):
         values = kvb[b, 1]
         kt = kvt[b, 0]
@@ -424,16 +429,18 @@
                     def _():
                         ry_copy(d).start()
 
-        @pl.when(b > NPB)
-        def _():
-            p = b - NPB - 1
-            gx_copy(p).wait()
-            zs[p] = (xs[p, c].astype(F32) + xr[p].astype(F32)).astype(BF)
-            gz_copy(p).start()
+        @pl.when(b > NPB + 1)
+        def _():
+            pass_on(b - NPB - 2)
 
         return carry
 
     lax.fori_loop(0, nb, grad_body, 0)
+
+    @pl.when(z > 0)
+    def _():
+        pass_on(z - 1)
+
 
     total = prom_s[c, y].astype(F32)
     for d in range(1, Y):

time: 47 us -> 47 us (level)
  no operation moved by 1% of the time
where the time goes in v6:
time: 47 us; the launch traced here: 46.1 us
  Pallas kernels  45.4 us (97%)
  between operations  0.64 us (1%)
    pallas_call x1, Pallas kernels, per_device(): pl.pallas_call(functools.partial(kernel, dims), out_shape=shapes, in_spec...  43.6 us
    pallas_call x1, Pallas kernels, per_device(): pl.pallas_call(write_out, out_shape=shapes, in_specs=[any_spec] * 6, out_...  1.86 us

profile of v6, /device:TPU:1, one launch (start us, length us, event | category | flops | bytes accessed | tf_op | source)
XLA Modules:
  0.0 46.1 jit_solution(9783810028186454389)
XLA Ops:
  0.6 43.6 %shard_map.118 = (bf16[128,1024]{1,0:T(8,128)(2,1)}, bf16[128,1024]{1,0:T(8,128)(2,1)}, bf16[128,128]{1,0:T(8,128)(2,1)}, bf16[128,128]{1,0:T(8,128)(2,1)}, f32[8,128]{1,0:T(8,128)}, /*index=5*/f32[8,128]{1,0:T(8,128)}) custom-call(bf16[16,8192]{1,0:T(8,128)(2,1)} %q_hbm.1, bf16[16,1024]{1,0:T(8,128)(2,1)} %k_hbm.1, bf16[16,1024]{1,0:T(8,128)(2,1)} %v_hbm.1, ...), custom_call_target="tpu_custom_call" | custom-call | tf_op jit(solution)/shard_map/pallas_call | solution.py:551
  44.2 1.9 %shard_map.119 = (bf16[128,1024]{1,0:T(8,128)(2,1)}, bf16[128,1024]{1,0:T(8,128)(2,1)}, bf16[128,128]{1,0:T(8,128)(2,1)}, bf16[128,128]{1,0:T(8,128)(2,1)}, f32[8,128]{1,0:T(8,128)}, /*index=5*/f32[8,128]{1,0:T(8,128)}) custom-call(bf16[128,1024]{1,0:T(8,128)(2,1)} %get-tuple-element.12.refs_0_, bf16[128,1024]{1,0:T(8,128)(2,1)} %get-tuple-element.13.refs_1_, ...), custom_call_target="tpu_custom_call" | custom-call | tf_op jit(solution)/shard_map/pallas_call | solution.py:617
